TPU v7x, 32 devices: a whole 2x2x4 slice. The times are simulated.
32 devices in a mesh: role: 2 (over core), dp: 4 (over z), vocab: 4 (over y, x).
Axes of the slice: x: 2, y: 2, z: 4, core: 2. Of those that a mesh axis runs over, the one named last changes fastest.
Arguments:
- teacher_hidden: bfloat16 [256, 4608], P('dp', ('role', 'vocab'))
- student_hidden: bfloat16 [256, 4096], P('dp', ('role', 'vocab'))
- teacher_unembed: bfloat16 [4608, 16384], P('role', ('dp', 'vocab')), may hold values from -6 to 6
- student_unembed: bfloat16 [4096, 16384], P('role', ('dp', 'vocab')), may hold values from -6 to 6
- targets: int32 [256], replicated, may hold values from 0 to 16383
Outputs:
- row_loss: float32 [256], replicated
- mean_loss: float32 [], replicated
- grad_hidden: float32 [256, 4096], P('dp', ('role', 'vocab'))
All inputs are finite; a program needn't handle non-finite values.
Results may differ from a plain program's by a relative error of at most 0.0017.
Values may be sent and summed in bfloat16 or wider, within the bound.
A program may use at most 64 MiB of HBM per device.

v0:
```python
import jax
import jax.numpy as jnp
from jax import lax
from jax.sharding import PartitionSpec as P


def shifted(value, axis, steps):
    count = lax.axis_size(axis)
    leading, last = (max(0, -steps), min(count, count - steps))
    return lax.ppermute(value, axis, [(source, source + steps) for source in range(leading, last)])


def normalize(logits):
    top = lax.pmax(jnp.max(logits, axis=-1), ("dp", "vocab"))
    total = lax.psum(jnp.sum(jnp.exp(logits - top[..., None]), axis=-1), ("dp", "vocab"))
    return logits - (top + jnp.log(total))[..., None]


def per_device(teacher_hidden, student_hidden, teacher_unembed, student_unembed, targets):
    teacher_half, student_half = (
        lax.all_gather(teacher_hidden, "vocab", axis=1, tiled=True),
        lax.all_gather(student_hidden, "vocab", axis=1, tiled=True),
    )
    row_count = teacher_half.shape[0] * lax.axis_size("dp")
    vocab_cols = teacher_unembed.shape[1]
    teacher_part = jnp.dot(
        lax.all_gather(teacher_half, "dp", axis=0, tiled=True),
        teacher_unembed,
        preferred_element_type=jnp.float32,
    )
    student_part = jnp.dot(
        lax.all_gather(student_half, "dp", axis=0, tiled=True),
        student_unembed,
        preferred_element_type=jnp.float32,
    )
    partial_logits = jnp.stack([teacher_part, student_part])
    is_student = (lax.axis_index("role") == 1).astype(jnp.float32)
    offset = (lax.axis_index("dp") * lax.axis_size("vocab") + lax.axis_index("vocab")) * vocab_cols
    column = lax.broadcasted_iota(jnp.int32, (1, vocab_cols), 1) + offset
    onehot = (column == targets[:, None]).astype(jnp.float32)
    logits = lax.psum_scatter(partial_logits, "role", scatter_dimension=0, tiled=True)[0]
    log_probs = normalize(logits)
    teacher_logp = shifted(log_probs, "role", 1)
    teacher_prob = jnp.exp(teacher_logp)
    student_prob = jnp.exp(log_probs)
    loss_part = (
        jnp.sum(teacher_prob * (teacher_logp - log_probs) - onehot * log_probs, axis=1) * is_student
    )
    own_grad = ((2.0 * student_prob - teacher_prob - onehot) * is_student).astype(jnp.bfloat16)
    passed_grad = shifted(own_grad, "role", -1)
    logit_grad = own_grad + passed_grad
    row_loss = lax.psum(loss_part, ("role", "dp", "vocab"))
    mean_loss = jnp.mean(row_loss)
    term = lax.dot_general(
        logit_grad, student_unembed, (((1,), (1,)), ((), ())), preferred_element_type=jnp.float32
    )
    dp_size = lax.axis_size("dp")
    vocab_size = lax.axis_size("vocab")
    group_rows = row_count // dp_size
    feature_cols = term.shape[1] // vocab_size
    arranged = term.reshape(dp_size, group_rows, vocab_size, feature_cols)
    arranged = arranged.transpose(0, 2, 1, 3).reshape(
        dp_size * vocab_size * group_rows, feature_cols
    )
    grad_hidden = lax.psum_scatter(arranged, ("dp", "vocab"), scatter_dimension=0, tiled=True)
    return (row_loss, mean_loss, grad_hidden)


def solution(mesh):
    return jax.shard_map(
        per_device,
        mesh=mesh,
        in_specs=(
            P("dp", ("role", "vocab")),
            P("dp", ("role", "vocab")),
            P("role", ("dp", "vocab")),
            P("role", ("dp", "vocab")),
            P(),
        ),
        out_specs=(P(), P(), P("dp", ("role", "vocab"))),
        check_vma=False,
    )
```

profile of v0, /device:TPU:0, one launch (start us, length us, event | category | flops | bytes accessed | tf_op | source)
XLA Modules:
  0.0 279.1 jit_solution(4261632622849662009)
XLA Ops:
  7.2 12.0 %all_gather.14 = bf16[64,2048]{1,0:T(8,128)(2,1)} all-gather(bf16[64,512]{1,0:T(8,128)(2,1)} %param.6), channel_id=1, replica_groups=mesh['role'=2,'dp'=4,'vocab'=4] {'vocab'}, dimensions={1}, use_global_device_ids=true | all-gather | bytes 327680 | tf_op jit(solution)/shard_map/all_gather | solution.py:22
  19.3 9.0 %all-gather = bf16[4,576,64]{1,2,0:T(8,128)(2,1)S(1)} all-gather(bf16[1,576,64]{1,2,0:T(8,128)(2,1)} %bitcast.29), channel_id=1, replica_groups=mesh['role'=2,'dp'=4,'vocab'=4] {'vocab'}, dimensions={0}, use_global_device_ids=true | all-gather | bytes 368640 | tf_op jit(solution)/shard_map/all_gather | solution.py:21
  28.5 1.0 reshape.23
  29.5 18.0 %all-gather.6.cloned.1.call-done = bf16[256,2048]{1,0:T(8,128)(2,1)} async-done(((bf16[64,2048]{1,0:T(8,128)(2,1)}), bf16[256,2048]{1,0:T(8,128)(2,1)}) %all-gather.6.cloned.1.call-update) | async-done | bytes 1048592 | tf_op jit(solution)/shard_map/all_gather | solution.py:32
  47.6 3.8 %convolution_bitcast_fusion = f32[1,256,1024]{2,1,0:T(8,128)S(1)} fusion(bf16[256,2048]{1,0:T(8,128)(2,1)} %all-gather.6.cloned.1.call-done, bf16[2048,1024]{1,0:T(8,128)(2,1)} %param.8), kind=kOutput, calls=%fused_computation.1 | convolution fusion | flops 1073741824 | bytes 6291456 | tf_op jit(solution)/shard_map/dot_general | solution.py:31
  51.3 27.8 %all-gather.4.cloned.1.call-done = bf16[256,2304]{1,0:T(8,128)(2,1)} async-done(((bf16[64,2304]{1,0:T(8,128)(2,1)}), bf16[256,2304]{1,0:T(8,128)(2,1)}) %all-gather.4.cloned.1.call-update) | async-done | bytes 1179664 | tf_op jit(solution)/shard_map/all_gather | solution.py:27
  79.1 4.1 %convolution_bitcast_fusion.1 = f32[1,256,1024]{2,1,0:T(8,128)S(1)} fusion(bf16[256,2304]{1,0:T(8,128)(2,1)} %all-gather.4.cloned.1.call-done, bf16[2304,1024]{1,0:T(8,128)(2,1)} %param.7), kind=kOutput, calls=%fused_computation.2 | convolution fusion | flops 1207959552 | bytes 6946816 | tf_op jit(solution)/shard_map/dot_general | solution.py:26
  83.2 1.6 pad_maximum_fusion
  84.8 8.8 %reduce-scatter.3.cloned.1.call-done = f32[1,256,1024]{2,1,0:T(8,128)} async-done(((f32[2,256,1024]{2,1,0:T(8,128)}), f32[1,256,1024]{2,1,0:T(8,128)}) %reduce-scatter.3.cloned.1.call-update) | async-done | bytes 1048592 | tf_op jit(solution)/shard_map/reduce_scatter | solution.py:41
  93.7 1.4 reduce_max.9
  95.1 41.9 %pmax.7 = f32[256]{0:T(256)S(1)} all-reduce(f32[256]{0:T(256)S(1)} %reduce_max.9), channel_id=1, replica_groups=mesh['role'=2,'dp'=4,'vocab'=4] {'dp','vocab'}, use_global_device_ids=true, to_apply=%region_2.0 | all-reduce | flops 256 | bytes 2048 | tf_op jit(solution)/shard_map/pmax | solution.py:14
  137.1 1.5 fusion.6
  138.6 36.6 %psum.14 = f32[256]{0:T(256)S(1)} all-reduce(f32[256]{0:T(256)S(1)} %fusion.6), channel_id=1, replica_groups=mesh['role'=2,'dp'=4,'vocab'=4] {'dp','vocab'}, use_global_device_ids=true, to_apply=%region_4.0 | all-reduce | flops 256 | bytes 2048 | tf_op jit(solution)/shard_map/psum | solution.py:15
  175.3 1.4 collective-permute-start
  176.7 2.2 collective-permute-done
  178.9 0.7 fusion.4
  179.6 1.3 collective-permute-start.1
  180.9 2.5 collective-permute-done.1
  183.4 4.8 %fusion.7 = f32[256,2048]{1,0:T(8,128)} fusion(bf16[2048,1024]{1,0:T(8,128)(2,1)} %param.8, bf16[256,1024]{1,0:T(8,128)(2,1)S(1)} %get-tuple-element.3, bf16[256,1024]{1,0:T(8,128)(2,1)S(1)} %collective-permute-done.1), kind=kOutput, calls=%fused_computation.14 | convolution fusion | flops 1074003968 | bytes 7340032 | tf_op jit(solution)/shard_map/dot_general | solution.py:54
  188.2 2.7 reshape.20
  190.9 2.0 copy.12
  192.9 39.4 %psum.15 = f32[256]{0:T(256)S(1)} all-reduce(f32[256]{0:T(256)S(1)} %broadcast_multiply_fusion), channel_id=1, replica_groups=mesh['role'=2,'dp'=4,'vocab'=4] {'role','dp','vocab'}, use_global_device_ids=true, to_apply=%region_6.0 | all-reduce | flops 256 | bytes 2048 | tf_op jit(solution)/shard_map/psum | solution.py:52
  232.3 0.6 reduce_sum.29
  233.6 37.9 %reduce-scatter.5.cloned.1.call-done = f32[64,512]{1,0:T(8,128)} async-done(((f32[1024,512]{1,0:T(8,128)}), f32[64,512]{1,0:T(8,128)}) %reduce-scatter.5.cloned.1.call-update) | async-done | bytes 131088 | tf_op jit(solution)/shard_map/reduce_scatter | solution.py:65
  (19 shorter events, 0.7 us)
Async XLA Ops:
  7.2 40.4 %all-gather.6.cloned.1.call-start = ((), (), s32[]{:S(2)}) async-start(), calls=%async_computation.3 | async-start | bytes 1310720 | tf_op jit(solution)/shard_map/all_gather | solution.py:32
  19.2 59.9 %all-gather.4.cloned.1.call-start = ((), (), s32[]{:S(2)}) async-start(), calls=%async_computation.2 | async-start | bytes 1474560 | tf_op jit(solution)/shard_map/all_gather | solution.py:27
  29.5 64.2 %reduce-scatter.3.cloned.1.call-start = ((), (), s32[]{:S(2)}) async-start(), calls=%async_computation.4 | async-start | bytes 3145728 | tf_op jit(solution)/shard_map/reduce_scatter | solution.py:41
  84.8 94.1 %copy-start.2 = (s32[256]{0:T(256)S(1)}, s32[256]{0:T(256)}, u32[]{:S(2)}) copy-start(s32[256]{0:T(256)} %param.9) | copy-start | bytes 3076
  84.8 186.7 %reduce-scatter.5.cloned.1.call-start = ((), (), s32[]{:S(2)}) async-start(), calls=%async_computation.5 | async-start | bytes 2228224 | tf_op jit(solution)/shard_map/reduce_scatter | solution.py:65
  93.7 81.5 %copy-start = (f32[1,256,1024]{2,1,0:T(8,128)S(1)}, f32[1,256,1024]{2,1,0:T(8,128)}, u32[]{:S(2)}) copy-start(f32[1,256,1024]{2,1,0:T(8,128)} %reduce-scatter.3.cloned.1.call-done) | copy-start | bytes 3145732
  175.3 3.6 %collective-permute-start = (f32[256,1024]{1,0:T(8,128)S(1)}, f32[256,1024]{1,0:T(8,128)S(1)}, u32[]{:S(2)}, u32[]{:S(2)}) collective-permute-start(f32[256,1024]{1,0:T(8,128)S(1)} %bitcast_subtract_fusion), channel_id=1, source_target_pairs={{0,16},{1,17},{2,18},{3,19},{4,20},{5,21},{6,22},{7,23},{8,24},{9,... | collective-permute-start | bytes 3145736 | tf_op jit(solution)/shard_map/ppermute | solution.py:10
  179.6 3.8 %collective-permute-start.1 = (bf16[256,1024]{1,0:T(8,128)(2,1)S(1)}, bf16[256,1024]{1,0:T(8,128)(2,1)S(1)}, u32[]{:S(2)}, u32[]{:S(2)}) collective-permute-start(bf16[256,1024]{1,0:T(8,128)(2,1)S(1)} %get-tuple-element.3), channel_id=1, source_target_pairs={{16,0},{17,1},{18,2},{19,3},{20,4},{21,5},{22,6},{23,7},{24,8},{25... | collective-permute-start | bytes 1572872 | tf_op jit(solution)/shard_map/ppermute | solution.py:10
  232.3 39.2 %copy-start.1 = (f32[256]{0:T(256)}, f32[256]{0:T(256)S(1)}, u32[]{:S(2)}) copy-start(f32[256]{0:T(256)S(1)} %psum.15) | copy-start | bytes 3076
Sparse Core Ops, SparseCore 0:
  19.3 28.1 all-gather.5
  49.1 29.9 all-gather.3
  84.9 8.7 reduce-scatter.2
  193.0 78.3 reduce-scatter.4
where the time goes:
time: 280 us; the launch traced here: 279 us
  blocking collectives  139 us (50%)
  waiting for transfers between devices  97.3 us (35%)
  between operations  15.6 us (6%)
  matrix products  12.7 us (5%)
  other arithmetic  6 us (2%)
  local copies, waits for them, and re-layouts  5.93 us (2%)
  starting transfers between devices  2.81 us (1%)
    pmax x1, blocking collectives, normalize(): top = lax.pmax(jnp.max(logits, axis=-1), ('dp', 'vocab'))  41.9 us
    psum x1, blocking collectives, per_device(): row_loss = lax.psum(loss_part, ('role', 'dp', 'vocab'))  39.4 us
    reduce_scatter x1, waiting for transfers between devices, per_device(): lax.psum_scatter(arranged, ('dp', 'vocab'), scatter_dimension=0, tiled=True)  37.9 us
    psum x1, blocking collectives, normalize(): lax.psum(jnp.sum(jnp.exp(logits - top[..., None]), axis=-1), ('dp', 'voca...  36.6 us
    all_gather x1, waiting for transfers between devices, per_device(): lax.all_gather(teacher_half, 'dp', axis=0, tiled=True)  27.8 us
    all_gather x1, waiting for transfers between devices, per_device(): lax.all_gather(student_half, 'dp', axis=0, tiled=True)  18 us
    all_gather x1, blocking collectives, per_device(): lax.all_gather(student_hidden, 'vocab', axis=1, tiled=True)  12 us
    all_gather x1, blocking collectives, per_device(): lax.all_gather(teacher_hidden, 'vocab', axis=1, tiled=True)  8.95 us
  transfers between devices with their start and end apart: 6, of which 6 were waited for; matrix products, arithmetic and copies ran while one was open for 2% of the time, Pallas kernels for 0%

commit v1 on v0

v1 whole, which is shorter than its diff:
```python
import functools

import jax
import jax.numpy as jnp
from jax import lax
from jax.experimental import pallas as pl
from jax.experimental.pallas import tpu as pltpu
from jax.sharding import PartitionSpec as P

MESH = pl.DeviceIdType.MESH
TILE = 256
ROW_STEP = 32
LANES = 128


def flipped(index, bits, size):
    out, bit = index, 1
    while bit < size:
        if bits & bit:
            out = out + bit * (1 - 2 * lax.rem(lax.div(index, bit), 2))
        bit *= 2
    return out


def kernel(
    dp_size, vocab_size,
    th_ref, sh_ref, tw_ref, sw_ref, targets_ref,
    loss_ref, mean_ref, grad_ref,
    th, sh, tw, sw, t_acc, s_acc, t_other, s_other, target_col, stat_col, stats, losses, lse_col,
    logit_grad, term, from_vocab, to_dp, from_dp,
    local_sem, t_send, t_recv, s_send, s_recv, role_send, role_recv,
    stat_send, stat_recv, v_send, v_recv, d_send, d_recv,
):
    role, dp, vocab = lax.axis_index("role"), lax.axis_index("dp"), lax.axis_index("vocab")
    group = dp_size * vocab_size
    me = dp * vocab_size + vocab
    cols = tw.shape[1]
    block_rows = th_ref.shape[0]
    rows = dp_size * block_rows
    half = rows // 2
    features = sh_ref.shape[1]
    dps = [flipped(dp, k, dp_size) for k in range(dp_size)]
    vocabs = [flipped(vocab, k, vocab_size) for k in range(vocab_size)]
    partner = (1 - role, dp, vocab)
    sent = []

    def send(src, dst, send_sem, recv_sem, device):
        copy = pltpu.make_async_remote_copy(
            src_ref=src, dst_ref=dst, send_sem=send_sem, recv_sem=recv_sem,
            device_id=device, device_id_type=MESH,
        )
        copy.start()
        sent.append(copy)

    def arrived(dst, send_sem, recv_sem):
        pltpu.make_async_remote_copy(
            src_ref=dst, dst_ref=dst, send_sem=send_sem, recv_sem=recv_sem,
            device_id=partner, device_id_type=MESH,
        ).wait_recv()

    tw_copy = pltpu.make_async_copy(tw_ref, tw, local_sem.at[0])
    sw_copy = pltpu.make_async_copy(sw_ref, sw, local_sem.at[1])
    th_copy = pltpu.make_async_copy(th_ref, th.at[vocab, dp], local_sem.at[2])
    sh_copy = pltpu.make_async_copy(sh_ref, sh.at[vocab, dp], local_sem.at[3])
    for copy in (th_copy, sh_copy, tw_copy, sw_copy):
        copy.start()

    barrier = pltpu.get_barrier_semaphore()

    @pl.loop(1, group)
    def _(step):
        other = lax.rem(me + step, group)
        pl.semaphore_signal(
            barrier, inc=1,
            device_id=(role, lax.div(other, vocab_size), lax.rem(other, vocab_size)),
            device_id_type=MESH,
        )

    pl.semaphore_signal(barrier, inc=1, device_id=partner, device_id_type=MESH)
    pl.semaphore_wait(barrier, group)

    parts = ((th_ref, th, t_send, t_recv), (sh_ref, sh, s_send, s_recv))
    for source, held, send_sem, recv_sem in parts:
        for k in range(1, dp_size):
            send(
                source, held.at[vocab, dp], send_sem.at[0, k], recv_sem.at[vocab, dp],
                (role, dps[k], vocab),
            )
        for k in range(1, vocab_size):
            send(
                source, held.at[vocab, dp], send_sem.at[k, 0], recv_sem.at[vocab, dp],
                (role, dp, vocabs[k]),
            )

    target_col[...] = jnp.transpose(jnp.broadcast_to(targets_ref[...], (LANES, rows)))

    def pass_on(held, send_sem, recv_sem):
        for j in range(1, dp_size):
            slot = held.at[vocab, dps[j]]
            arrived(slot, send_sem.at[0, 0], recv_sem.at[vocab, dps[j]])
            for k in range(1, vocab_size):
                send(
                    slot, slot, send_sem.at[k, j], recv_sem.at[vocab, dps[j]],
                    (role, dp, vocabs[k]),
                )

    def add_product(held, weights, acc, k):
        depth = held.shape[-1]
        start = pl.multiple_of(vocabs[k] * depth, 16)

        @pl.loop(0, cols // TILE)
        def _(n):
            at = pl.ds(pl.multiple_of(n * TILE, TILE), TILE)
            product = jnp.dot(
                held[vocabs[k]].reshape(rows, depth),
                weights[pl.ds(start, depth), at],
                preferred_element_type=jnp.float32,
            )
            if k == 0:
                acc[:, at] = product
            else:
                acc[:, at] += product

    def add_arriving(held, weights, acc, send_sem, recv_sem):
        for k in range(1, vocab_size):
            for j in range(dp_size):
                arrived(
                    held.at[vocabs[k], dps[j]], send_sem.at[0, 0], recv_sem.at[vocabs[k], dps[j]]
                )
            add_product(held, weights, acc, k)

    own_rows = pl.multiple_of(role * half, ROW_STEP)
    other_rows = pl.multiple_of((1 - role) * half, ROW_STEP)

    pass_on(th, t_send, t_recv)
    th_copy.wait()
    tw_copy.wait()
    add_product(th, tw, t_acc, 0)
    pass_on(sh, s_send, s_recv)
    sh_copy.wait()
    sw_copy.wait()
    add_product(sh, sw, s_acc, 0)
    add_arriving(th, tw, t_acc, t_send, t_recv)
    send(t_acc.at[pl.ds(other_rows, half)], t_other, role_send.at[0], role_recv.at[0], partner)
    add_arriving(sh, sw, s_acc, s_send, s_recv)
    send(s_acc.at[pl.ds(other_rows, half)], s_other, role_send.at[1], role_recv.at[1], partner)
    arrived(t_other, role_send.at[0], role_recv.at[0])
    arrived(s_other, role_send.at[1], role_recv.at[1])

    column = lax.broadcasted_iota(jnp.int32, (ROW_STEP, cols), 1) + me * cols
    lane = lax.broadcasted_iota(jnp.int32, (ROW_STEP, LANES), 1)

    def at_rows(step):
        local = pl.ds(pl.multiple_of(step * ROW_STEP, ROW_STEP), ROW_STEP)
        whole = pl.ds(pl.multiple_of(own_rows + step * ROW_STEP, ROW_STEP), ROW_STEP)
        return local, whole

    @pl.loop(0, half // ROW_STEP)
    def _(step):
        local, whole = at_rows(step)
        teacher = t_acc[whole, :] + t_other[local, :]
        student = s_acc[whole, :] + s_other[local, :]
        hit = column == target_col[whole, 0:1]
        t_top = jnp.max(teacher, axis=1, keepdims=True)
        s_top = jnp.max(student, axis=1, keepdims=True)
        t_exp = jnp.exp(teacher - t_top)
        t_sum = jnp.sum(t_exp, axis=1, keepdims=True)
        gap = jnp.sum(t_exp * (teacher - student), axis=1, keepdims=True)
        s_sum = jnp.sum(jnp.exp(student - s_top), axis=1, keepdims=True)
        label = jnp.sum(jnp.where(hit, student, 0.0), axis=1, keepdims=True)
        packed = jnp.zeros((ROW_STEP, LANES), jnp.float32)
        for place, value in enumerate((t_top, t_sum, gap, s_top, s_sum, label)):
            packed = jnp.where(lane == place, value, packed)
        stat_col[local, :] = packed

    stats[me] = jnp.transpose(stat_col[...])[0:8, :]

    def stat_copy(step):
        other = lax.rem(me + step, group)
        return pltpu.make_async_remote_copy(
            src_ref=stats.at[me], dst_ref=stats.at[me],
            send_sem=stat_send.at[step], recv_sem=stat_recv.at[me],
            device_id=(role, lax.div(other, vocab_size), lax.rem(other, vocab_size)),
            device_id_type=MESH,
        )

    @pl.loop(1, group)
    def _(step):
        stat_copy(step).start()

    @pl.loop(1, group)
    def _(step):
        other = lax.rem(me + step, group)
        arrived(stats.at[other], stat_send.at[0], stat_recv.at[other])

    everyone = stats[...]
    t_top, t_sum, gap = everyone[:, 0, :], everyone[:, 1, :], everyone[:, 2, :]
    s_top, s_sum, label = everyone[:, 3, :], everyone[:, 4, :], everyone[:, 5, :]
    t_max = jnp.max(t_top, axis=0, keepdims=True)
    s_max = jnp.max(s_top, axis=0, keepdims=True)
    t_scale = jnp.exp(t_top - t_max)
    t_total = jnp.sum(t_sum * t_scale, axis=0, keepdims=True)
    s_total = jnp.sum(s_sum * jnp.exp(s_top - s_max), axis=0, keepdims=True)
    t_lse = t_max + jnp.log(t_total)
    s_lse = s_max + jnp.log(s_total)
    mean_gap = jnp.sum(gap * t_scale, axis=0, keepdims=True) / t_total
    s_label = jnp.sum(label, axis=0, keepdims=True)
    loss = (mean_gap - t_lse + s_lse) - (s_label - s_lse)
    losses[role] = jnp.broadcast_to(loss, (8, half))
    send(losses.at[role], losses.at[role], role_send.at[2], role_recv.at[2], partner)
    first = lax.broadcasted_iota(jnp.int32, (LANES, half), 0) == 0
    lse_col[...] = jnp.transpose(jnp.where(first, t_lse, s_lse))

    @pl.loop(0, half // ROW_STEP)
    def _(step):
        local, whole = at_rows(step)
        teacher = t_acc[whole, :] + t_other[local, :]
        student = s_acc[whole, :] + s_other[local, :]
        onehot = jnp.where(column == target_col[whole, 0:1], 1.0, 0.0)
        t_prob = jnp.exp(teacher - lse_col[local, 0:1])
        s_prob = jnp.exp(student - lse_col[local, 1:2])
        logit_grad[whole, :] = (2.0 * s_prob - t_prob - onehot).astype(jnp.bfloat16)

    mine = logit_grad.at[pl.ds(own_rows, half)]
    send(mine, mine, role_send.at[3], role_recv.at[3], partner)
    arrived(logit_grad.at[pl.ds(other_rows, half)], role_send.at[3], role_recv.at[3])

    def block(j):
        return pl.ds(pl.multiple_of(dps[j] * block_rows, block_rows), block_rows)

    def send_term(k, j):
        send(
            term.at[k, block(j)], from_vocab.at[k, block(j)],
            v_send.at[k, j], v_recv.at[k, dps[j]], (role, dp, vocabs[k]),
        )

    width = min(TILE, features)
    order = list(range(vocab_size - 1, -1, -1))
    far = list(range(dp_size - 1, -1, -1))
    for k in order:
        @pl.loop(0, features // width)
        def _(n):
            start = pl.multiple_of(vocabs[k] * features + n * width, width)
            term[k, :, pl.ds(pl.multiple_of(n * width, width), width)] = lax.dot_general(
                logit_grad[...], sw[pl.ds(start, width), :],
                (((1,), (1,)), ((), ())), preferred_element_type=jnp.float32,
            )
        if k:
            send_term(k, far[0])
    for j in far[1:]:
        for k in order[:-1]:
            send_term(k, j)
    for j in far:
        total = term[0, block(j), :]
        for k in order[:-1]:
            arrived(from_vocab.at[k, block(j)], v_send.at[0, 0], v_recv.at[k, dps[j]])
            total = total + from_vocab[k, block(j), :]
        to_dp[j] = total
        if j:
            send(to_dp.at[j], from_dp.at[j], d_send.at[j], d_recv.at[j], (role, dps[j], vocab))
    result = to_dp[0]
    for j in far[:-1]:
        arrived(from_dp.at[j], d_send.at[0], d_recv.at[j])
        result = result + from_dp[j]
    grad_ref[...] = result

    arrived(losses.at[1 - role], role_send.at[2], role_recv.at[2])
    both = losses[:, 0, :]
    loss_ref[...] = both
    mean_ref[...] = jnp.sum(jnp.sum(both, axis=1, keepdims=True), axis=0, keepdims=True) * (1.0 / rows)

    for copy in sent:
        copy.wait_send()

    @pl.loop(1, group)
    def _(step):
        stat_copy(step).wait_send()


def per_device(dp_size, vocab_size, teacher_hidden, student_hidden, teacher_unembed, student_unembed, targets):
    block_rows, t_depth = teacher_hidden.shape
    s_depth = student_hidden.shape[1]
    rows = dp_size * block_rows
    half = rows // 2
    cols = teacher_unembed.shape[1]
    group = dp_size * vocab_size
    f32, bf16 = jnp.float32, jnp.bfloat16
    vmem, dma = pltpu.VMEM, pltpu.SemaphoreType.DMA
    any_spec = pl.BlockSpec(memory_space=pl.ANY)
    vmem_spec = pl.BlockSpec(memory_space=pltpu.VMEM)
    losses, mean, grad = pl.pallas_call(
        functools.partial(kernel, dp_size, vocab_size),
        out_shape=(
            jax.ShapeDtypeStruct((2, half), f32),
            jax.ShapeDtypeStruct((1, 1), f32),
            jax.ShapeDtypeStruct((block_rows, s_depth), f32),
        ),
        in_specs=[any_spec] * 4 + [vmem_spec],
        out_specs=(vmem_spec,) * 3,
        scratch_shapes=[
            vmem((vocab_size, dp_size, block_rows, t_depth), bf16),
            vmem((vocab_size, dp_size, block_rows, s_depth), bf16),
            vmem(teacher_unembed.shape, bf16),
            vmem(student_unembed.shape, bf16),
            vmem((rows, cols), f32),
            vmem((rows, cols), f32),
            vmem((half, cols), f32),
            vmem((half, cols), f32),
            vmem((rows, LANES), jnp.int32),
            vmem((half, LANES), f32),
            vmem((group, 8, half), f32),
            vmem((2, 8, half), f32),
            vmem((half, LANES), f32),
            vmem((rows, cols), bf16),
            vmem((vocab_size, rows, s_depth), f32),
            vmem((vocab_size, rows, s_depth), f32),
            vmem((dp_size, block_rows, s_depth), f32),
            vmem((dp_size, block_rows, s_depth), f32),
            dma((4,)),
            dma((vocab_size, dp_size)),
            dma((vocab_size, dp_size)),
            dma((vocab_size, dp_size)),
            dma((vocab_size, dp_size)),
            dma((4,)),
            dma((4,)),
            dma((group,)),
            dma((group,)),
            dma((vocab_size, dp_size)),
            dma((vocab_size, dp_size)),
            dma((dp_size,)),
            dma((dp_size,)),
        ],
        compiler_params=pltpu.CompilerParams(
            collective_id=0, has_side_effects=True, vmem_limit_bytes=50 * 1024 * 1024
        ),
    )(teacher_hidden, student_hidden, teacher_unembed, student_unembed, targets.reshape(1, rows))
    return losses.reshape(rows), mean.reshape(()), grad


def solution(mesh):
    return jax.shard_map(
        functools.partial(per_device, mesh.shape["dp"], mesh.shape["vocab"]),
        mesh=mesh,
        in_specs=(
            P("dp", ("role", "vocab")),
            P("dp", ("role", "vocab")),
            P("role", ("dp", "vocab")),
            P("role", ("dp", "vocab")),
            P(),
        ),
        out_specs=(P(), P(), P("dp", ("role", "vocab"))),
        check_vma=False,
    )
```

time: 280 us -> 77.5 us (0.28)
  blocking collectives: 139 us -> 0 us
  waiting for transfers between devices: 97.3 us -> 0 us
  Pallas kernels: 0 us -> 71.3 us
  between operations: 15.6 us -> 2.39 us
  matrix products: 12.7 us -> 0 us
  other arithmetic: 6 us -> 0 us
  starting transfers between devices: 2.81 us -> 0 us
    psum x2 -> x0, blocking collectives: 75.9 us -> none  [the longest x1 39.4 us: per_device(): row_loss = lax.psum(loss_part, ('role', 'dp', 'vocab'))]
    pallas_call x0 -> x1, Pallas kernels: none -> 71.3 us  [per_device(): pl.pallas_call(functools.partial(kernel, dp_size, vocab_size), out_shape=...]
    reduce_scatter x2 -> x0, waiting for transfers between devices: 46.7 us -> none  [the longest x1 37.9 us: per_device(): lax.psum_scatter(arranged, ('dp', 'vocab'), scatter_dimension=0, tiled=True)]
    all_gather x2 -> x0, waiting for transfers between devices: 45.8 us -> none  [the longest x1 27.8 us: per_device(): lax.all_gather(teacher_half, 'dp', axis=0, tiled=True)]
    pmax x1 -> x0, blocking collectives: 41.9 us -> none  [normalize(): top = lax.pmax(jnp.max(logits, axis=-1), ('dp', 'vocab'))]
    all_gather x2 -> x0, blocking collectives: 20.9 us -> none  [the longest x1 12 us: per_device(): lax.all_gather(student_hidden, 'vocab', axis=1, tiled=True)]
    dot_general x3 -> x0, matrix products: 12.7 us -> none  [the longest x1 4.83 us: per_device(): lax.dot_general(logit_grad, student_unembed, (((1,), (1,)), ((), ())), pr...]
    ppermute x2 -> x0, waiting for transfers between devices: 4.69 us -> none  [shifted(): lax.ppermute(value, axis, [(source, source + steps) for source in range(l...]
  transfers between devices with their start and end apart: 6 -> 0, of which waited for: 6 -> 0; matrix products, arithmetic and copies ran while one was open for 2% -> 0% of each run, Pallas kernels for 0% -> 0%
where the time goes in v1:
time: 77.5 us; the launch traced here: 77.3 us
  Pallas kernels  71.3 us (92%)
  local copies, waits for them, and re-layouts  3.62 us (5%)
  between operations  2.39 us (3%)
    pallas_call x1, Pallas kernels, per_device(): pl.pallas_call(functools.partial(kernel, dp_size, vocab_size), out_shape=...  71.3 us
    unnamed x8, local copies, waits for them, and re-layouts  3.62 us

profile of v1, /device:TPU:0, one launch (start us, length us, event | category | flops | bytes accessed | tf_op | source)
XLA Modules:
  0.0 77.3 jit_solution(9570839096242196350)
XLA Ops:
  0.6 0.0 copy-start
  0.6 0.9 %copy-done = bf16[64,576]{1,0:T(8,128)(2,1)S(1)} copy-done((bf16[64,576]{1,0:T(8,128)(2,1)S(1)}, bf16[64,576]{1,0:T(8,128)(2,1)}, u32[]{:S(2)}) %copy-start) | copy-done | bytes 73752
  1.5 0.0 copy-start.1
  1.5 0.8 %copy-done.1 = bf16[64,512]{1,0:T(8,128)(2,1)S(1)} copy-done((bf16[64,512]{1,0:T(8,128)(2,1)S(1)}, bf16[64,512]{1,0:T(8,128)(2,1)}, u32[]{:S(2)}) %copy-start.1) | copy-done | bytes 65560
  2.4 0.0 copy-start.2
  2.4 0.7 copy-done.2
  3.0 71.3 %shard_map.76 = (f32[2,128]{1,0:T(2,128)S(1)}, f32[1,1]{1,0:T(1,128)}, f32[64,512]{1,0:T(8,128)S(1)}) custom-call(bf16[64,576]{1,0:T(8,128)(2,1)S(1)} %copy-done, bf16[64,512]{1,0:T(8,128)(2,1)S(1)} %copy-done.1, bf16[2304,1024]{1,0:T(8,128)(2,1)} %tw_ref.1, bf16[2048,1024]{1,0:T(8,128)(2,1)} %sw_ref.1, s32[1,256]{1,0:T(1,128)S(1)} %bitcast.3), custom_call_target="tpu_custom_call" | custom-call | tf_op jit(solution)/shard_map/pallas_call | solution.py:291
  74.3 0.6 copy.11
  75.5 0.7 copy.13
Async XLA Ops:
  0.6 0.9 %copy-start = (bf16[64,576]{1,0:T(8,128)(2,1)S(1)}, bf16[64,576]{1,0:T(8,128)(2,1)}, u32[]{:S(2)}) copy-start(bf16[64,576]{1,0:T(8,128)(2,1)} %th_ref.1) | copy-start | bytes 221188
  1.5 0.8 %copy-start.1 = (bf16[64,512]{1,0:T(8,128)(2,1)S(1)}, bf16[64,512]{1,0:T(8,128)(2,1)}, u32[]{:S(2)}) copy-start(bf16[64,512]{1,0:T(8,128)(2,1)} %sh_ref.1) | copy-start | bytes 196612
  2.4 0.7 copy-start.2

commit v2 on v1

--- a/solution.py
+++ b/solution.py
@@ -11,6 +11,7 @@
 TILE = 256
 ROW_STEP = 32
 LANES = 128
+HOP = jnp.float32
 
 
 def flipped(index, bits, size):
@@ -26,10 +27,10 @@
     dp_size, vocab_size,
     th_ref, sh_ref, tw_ref, sw_ref, targets_ref,
     loss_ref, mean_ref, grad_ref,
-    th, sh, tw, sw, t_acc, s_acc, t_other, s_other, target_col, stat_col, stats, losses, lse_col,
-    logit_grad, term, from_vocab, to_dp, from_dp,
+    th, sh, tw, sw, targets, t_acc, s_acc, t_other, s_other, target_col, stat_col, stats, losses, lse_col,
+    logit_grad, term, from_vocab, out_hop, in_hop, middle, in_last, to_dp, from_dp,
     local_sem, t_send, t_recv, s_send, s_recv, role_send, role_recv,
-    stat_send, stat_recv, v_send, v_recv, d_send, d_recv,
+    stat_send, stat_recv, v_send, v_recv, h_send, h_recv, d_send, d_recv,
 ):
     role, dp, vocab = lax.axis_index("role"), lax.axis_index("dp"), lax.axis_index("vocab")
     group = dp_size * vocab_size
@@ -62,47 +63,60 @@
     sw_copy = pltpu.make_async_copy(sw_ref, sw, local_sem.at[1])
     th_copy = pltpu.make_async_copy(th_ref, th.at[vocab, dp], local_sem.at[2])
     sh_copy = pltpu.make_async_copy(sh_ref, sh.at[vocab, dp], local_sem.at[3])
-    for copy in (th_copy, sh_copy, tw_copy, sw_copy):
+    targets_copy = pltpu.make_async_copy(targets_ref, targets, local_sem.at[4])
+    for copy in (th_copy, sh_copy, tw_copy, sw_copy, targets_copy):
         copy.start()
 
     barrier = pltpu.get_barrier_semaphore()
 
-    @pl.loop(1, group)
-    def _(step):
-        other = lax.rem(me + step, group)
-        pl.semaphore_signal(
-            barrier, inc=1,
-            device_id=(role, lax.div(other, vocab_size), lax.rem(other, vocab_size)),
-            device_id_type=MESH,
-        )
-
-    pl.semaphore_signal(barrier, inc=1, device_id=partner, device_id_type=MESH)
-    pl.semaphore_wait(barrier, group)
-
-    parts = ((th_ref, th, t_send, t_recv), (sh_ref, sh, s_send, s_recv))
-    for source, held, send_sem, recv_sem in parts:
+    neighbours = [(role, dps[k], vocab) for k in range(1, dp_size)]
+    neighbours += [(role, dp, vocabs[k]) for k in range(1, vocab_size)]
+    for neighbour in neighbours + [partner]:
+        pl.semaphore_signal(barrier, inc=1, device_id=neighbour, device_id_type=MESH)
+    pl.semaphore_wait(barrier, dp_size + vocab_size - 1)
+
+    corner = vocab_size == 4
+    direct = (1, 2) if corner else tuple(range(1, vocab_size))
+    teacher_part = (th, t_send, t_recv)
+    student_part = (sh, s_send, s_recv)
+    for source, (held, send_sem, recv_sem) in ((th_ref, teacher_part), (sh_ref, student_part)):
         for k in range(1, dp_size):
             send(
                 source, held.at[vocab, dp], send_sem.at[0, k], recv_sem.at[vocab, dp],
                 (role, dps[k], vocab),
             )
-        for k in range(1, vocab_size):
+        for k in direct:
             send(
                 source, held.at[vocab, dp], send_sem.at[k, 0], recv_sem.at[vocab, dp],
                 (role, dp, vocabs[k]),
             )
 
-    target_col[...] = jnp.transpose(jnp.broadcast_to(targets_ref[...], (LANES, rows)))
-
-    def pass_on(held, send_sem, recv_sem):
-        for j in range(1, dp_size):
-            slot = held.at[vocab, dps[j]]
-            arrived(slot, send_sem.at[0, 0], recv_sem.at[vocab, dps[j]])
-            for k in range(1, vocab_size):
-                send(
-                    slot, slot, send_sem.at[k, j], recv_sem.at[vocab, dps[j]],
-                    (role, dp, vocabs[k]),
-                )
+    targets_copy.wait()
+    target_col[...] = jnp.transpose(jnp.broadcast_to(targets[...], (LANES, rows)))
+
+    def pass_on(part, j):
+        held, send_sem, recv_sem = part
+        slot = held.at[vocab, dps[j]]
+        arrived(slot, send_sem.at[0, 0], recv_sem.at[vocab, dps[j]])
+        for k in direct:
+            send(
+                slot, slot, send_sem.at[k, j], recv_sem.at[vocab, dps[j]],
+                (role, dp, vocabs[k]),
+            )
+
+    def relay(part, j):
+        if not corner:
+            return
+        held, send_sem, recv_sem = part
+        middle = block_rows // 2
+        for k, at in ((1, pl.ds(0, middle)), (2, pl.ds(middle, middle))):
+            slot = (vocabs[k], dps[j])
+            arrived(held.at[slot], send_sem.at[0, 0], recv_sem.at[slot])
+            piece = held.at[slot[0], slot[1], at]
+            send(
+                piece, piece, send_sem.at[vocab_size + k - 1, j], recv_sem.at[slot],
+                (role, dp, vocabs[3 - k]),
+            )
 
     def add_product(held, weights, acc, k):
         depth = held.shape[-1]
@@ -121,28 +135,38 @@
             else:
                 acc[:, at] += product
 
-    def add_arriving(held, weights, acc, send_sem, recv_sem):
-        for k in range(1, vocab_size):
-            for j in range(dp_size):
-                arrived(
-                    held.at[vocabs[k], dps[j]], send_sem.at[0, 0], recv_sem.at[vocabs[k], dps[j]]
-                )
+    def add_arriving(part, weights, acc, ks):
+        held, send_sem, recv_sem = part
+        for k in ks:
+            if k == 3 or not corner:
+                for j in range(dp_size):
+                    slot = (vocabs[k], dps[j])
+                    arrived(held.at[slot], send_sem.at[0, 0], recv_sem.at[slot])
             add_product(held, weights, acc, k)
 
     own_rows = pl.multiple_of(role * half, ROW_STEP)
     other_rows = pl.multiple_of((1 - role) * half, ROW_STEP)
 
-    pass_on(th, t_send, t_recv)
+    for j in range(1, dp_size):
+        pass_on(teacher_part, j)
     th_copy.wait()
     tw_copy.wait()
     add_product(th, tw, t_acc, 0)
-    pass_on(sh, s_send, s_recv)
+    relay(teacher_part, 0)
+    for j in range(1, dp_size):
+        relay(teacher_part, j)
+        pass_on(student_part, j)
     sh_copy.wait()
     sw_copy.wait()
+    for j in range(dp_size):
+        relay(student_part, j)
     add_product(sh, sw, s_acc, 0)
-    add_arriving(th, tw, t_acc, t_send, t_recv)
+    early, late = ((1, 2), (3,)) if corner else ((), direct)
+    add_arriving(teacher_part, tw, t_acc, early)
+    add_arriving(student_part, sw, s_acc, early)
+    add_arriving(teacher_part, tw, t_acc, late)
     send(t_acc.at[pl.ds(other_rows, half)], t_other, role_send.at[0], role_recv.at[0], partner)
-    add_arriving(sh, sw, s_acc, s_send, s_recv)
+    add_arriving(student_part, sw, s_acc, late)
     send(s_acc.at[pl.ds(other_rows, half)], s_other, role_send.at[1], role_recv.at[1], partner)
     arrived(t_other, role_send.at[0], role_recv.at[0])
     arrived(s_other, role_send.at[1], role_recv.at[1])
@@ -234,30 +258,86 @@
             v_send.at[k, j], v_recv.at[k, dps[j]], (role, dp, vocabs[k]),
         )
 
-    width = min(TILE, features)
-    order = list(range(vocab_size - 1, -1, -1))
     far = list(range(dp_size - 1, -1, -1))
-    for k in order:
-        @pl.loop(0, features // width)
-        def _(n):
-            start = pl.multiple_of(vocabs[k] * features + n * width, width)
-            term[k, :, pl.ds(pl.multiple_of(n * width, width), width)] = lax.dot_general(
-                logit_grad[...], sw[pl.ds(start, width), :],
-                (((1,), (1,)), ((), ())), preferred_element_type=jnp.float32,
-            )
-        if k:
-            send_term(k, far[0])
-    for j in far[1:]:
-        for k in order[:-1]:
-            send_term(k, j)
-    for j in far:
-        total = term[0, block(j), :]
-        for k in order[:-1]:
-            arrived(from_vocab.at[k, block(j)], v_send.at[0, 0], v_recv.at[k, dps[j]])
-            total = total + from_vocab[k, block(j), :]
+
+    def product(k, n, width):
+        start = pl.multiple_of(vocabs[k] * features + n * width, width)
+        return lax.dot_general(
+            logit_grad[...], sw[pl.ds(start, width), :],
+            (((1,), (1,)), ((), ())), preferred_element_type=jnp.float32,
+        )
+
+    def finish(j, total):
         to_dp[j] = total
         if j:
             send(to_dp.at[j], from_dp.at[j], d_send.at[j], d_recv.at[j], (role, dps[j], vocab))
+
+    if corner:
+        width = features // 2
+        sides = (pl.ds(0, width), pl.ds(width, width))
+
+        def hop(side, slot, j):
+            send(
+                out_hop.at[side, slot, block(j)], in_hop.at[side, slot, block(j)],
+                h_send.at[side, slot, j], h_recv.at[side, slot, dps[j]],
+                (role, dp, vocabs[1 + side]),
+            )
+
+        def landed(buffer, side, slot, j):
+            arrived(
+                buffer.at[side, slot, block(j)] if slot < 2 else buffer.at[side, block(j)],
+                h_send.at[0, 0, 0], h_recv.at[side, slot, dps[j]],
+            )
+
+        for side in (0, 1):
+            out_hop[side, 1] = product(3, side, width).astype(HOP)
+            for j in far:
+                hop(side, 1, j)
+        for side in (0, 1):
+            out_hop[side, 0] = product(1 + side, side, width).astype(HOP)
+            hop(side, 0, far[0])
+        for side in (0, 1):
+            middle[side] = product(2 - side, side, width)
+        for side in (0, 1):
+            term[0, :, sides[side]] = product(0, side, width)
+        for at, j in enumerate(far):
+            for side in (0, 1):
+                landed(in_hop, side, 1, j)
+                middle[side, block(j)] += in_hop[side, 1, block(j)].astype(jnp.float32)
+                send(
+                    middle.at[side, block(j)], in_last.at[side, block(j)],
+                    h_send.at[side, 2, j], h_recv.at[side, 2, dps[j]],
+                    (role, dp, vocabs[2 - side]),
+                )
+            if at + 1 < dp_size:
+                for side in (0, 1):
+                    hop(side, 0, far[at + 1])
+        for j in far:
+            totals = []
+            for side in (0, 1):
+                landed(in_hop, side, 0, j)
+                near = term[0, block(j), sides[side]] + in_hop[side, 0, block(j)].astype(jnp.float32)
+                landed(in_last, side, 2, j)
+                totals.append(near + in_last[side, block(j)])
+            finish(j, jnp.concatenate(totals, axis=1))
+    else:
+        width = min(TILE, features)
+        order = list(range(vocab_size - 1, -1, -1))
+        for k in order:
+            @pl.loop(0, features // width)
+            def _(n):
+                term[k, :, pl.ds(pl.multiple_of(n * width, width), width)] = product(k, n, width)
+            if k:
+                send_term(k, far[0])
+        for j in far[1:]:
+            for k in order[:-1]:
+                send_term(k, j)
+        for j in far:
+            total = term[0, block(j), :]
+            for k in order[:-1]:
+                arrived(from_vocab.at[k, block(j)], v_send.at[0, 0], v_recv.at[k, dps[j]])
+                total = total + from_vocab[k, block(j), :]
+            finish(j, total)
     result = to_dp[0]
     for j in far[:-1]:
         arrived(from_dp.at[j], d_send.at[0], d_recv.at[j])
@@ -284,9 +364,11 @@
     half = rows // 2
     cols = teacher_unembed.shape[1]
     group = dp_size * vocab_size
+    corner = vocab_size == 4
+    hop_rows = rows if corner else 16
     f32, bf16 = jnp.float32, jnp.bfloat16
     vmem, dma = pltpu.VMEM, pltpu.SemaphoreType.DMA
-    any_spec = pl.BlockSpec(memory_space=pl.ANY)
+    any_spec = pl.BlockSpec(memory_space=pltpu.HBM)
     vmem_spec = pl.BlockSpec(memory_space=pltpu.VMEM)
     losses, mean, grad = pl.pallas_call(
         functools.partial(kernel, dp_size, vocab_size),
@@ -295,13 +377,14 @@
             jax.ShapeDtypeStruct((1, 1), f32),
             jax.ShapeDtypeStruct((block_rows, s_depth), f32),
         ),
-        in_specs=[any_spec] * 4 + [vmem_spec],
+        in_specs=[any_spec] * 5,
         out_specs=(vmem_spec,) * 3,
         scratch_shapes=[
             vmem((vocab_size, dp_size, block_rows, t_depth), bf16),
             vmem((vocab_size, dp_size, block_rows, s_depth), bf16),
             vmem(teacher_unembed.shape, bf16),
             vmem(student_unembed.shape, bf16),
+            vmem((1, rows), jnp.int32),
             vmem((rows, cols), f32),
             vmem((rows, cols), f32),
             vmem((half, cols), f32),
@@ -312,14 +395,18 @@
             vmem((2, 8, half), f32),
             vmem((half, LANES), f32),
             vmem((rows, cols), bf16),
-            vmem((vocab_size, rows, s_depth), f32),
-            vmem((vocab_size, rows, s_depth), f32),
+            vmem((1 if corner else vocab_size, rows, s_depth), f32),
+            vmem((1 if corner else vocab_size, 8 if corner else rows, s_depth), f32),
+            vmem((2, 2, hop_rows, s_depth // 2), HOP),
+            vmem((2, 2, hop_rows, s_depth // 2), HOP),
+            vmem((2, hop_rows, s_depth // 2), f32),
+            vmem((2, hop_rows, s_depth // 2), f32),
             vmem((dp_size, block_rows, s_depth), f32),
             vmem((dp_size, block_rows, s_depth), f32),
-            dma((4,)),
+            dma((5,)),
+            dma((vocab_size + 2, dp_size)),
             dma((vocab_size, dp_size)),
-            dma((vocab_size, dp_size)),
-            dma((vocab_size, dp_size)),
+            dma((vocab_size + 2, dp_size)),
             dma((vocab_size, dp_size)),
             dma((4,)),
             dma((4,)),
@@ -327,6 +414,8 @@
             dma((group,)),
             dma((vocab_size, dp_size)),
             dma((vocab_size, dp_size)),
+            dma((2, 3, dp_size)),
+            dma((2, 3, dp_size)),
             dma((dp_size,)),
             dma((dp_size,)),
         ],

time: 77.5 us -> 74 us (0.955)
  Pallas kernels: 71.3 us -> 67.8 us
    pallas_call x1, Pallas kernels: 71.3 us -> 67.8 us  [per_device(): pl.pallas_call(functools.partial(kernel, dp_size, vocab_size), out_shape=...]
where the time goes in v2:
time: 74 us; the launch traced here: 73.8 us
  Pallas kernels  67.8 us (92%)
  local copies, waits for them, and re-layouts  3.62 us (5%)
  between operations  2.39 us (3%)
    pallas_call x1, Pallas kernels, per_device(): pl.pallas_call(functools.partial(kernel, dp_size, vocab_size), out_shape=...  67.8 us
    unnamed x8, local copies, waits for them, and re-layouts  3.62 us

profile of v2, /device:TPU:0, one launch (start us, length us, event | category | flops | bytes accessed | tf_op | source)
XLA Modules:
  0.0 73.8 jit_solution(11695592304441951838)
XLA Ops:
  0.6 0.0 copy-start
  0.6 0.9 %copy-done = bf16[64,576]{1,0:T(8,128)(2,1)S(1)} copy-done((bf16[64,576]{1,0:T(8,128)(2,1)S(1)}, bf16[64,576]{1,0:T(8,128)(2,1)}, u32[]{:S(2)}) %copy-start) | copy-done | bytes 73752
  1.5 0.0 copy-start.1
  1.5 0.8 %copy-done.1 = bf16[64,512]{1,0:T(8,128)(2,1)S(1)} copy-done((bf16[64,512]{1,0:T(8,128)(2,1)S(1)}, bf16[64,512]{1,0:T(8,128)(2,1)}, u32[]{:S(2)}) %copy-start.1) | copy-done | bytes 65560
  2.4 0.0 copy-start.2
  2.4 0.7 copy-done.2
  3.0 67.8 %shard_map.76 = (f32[2,128]{1,0:T(2,128)S(1)}, f32[1,1]{1,0:T(1,128)}, f32[64,512]{1,0:T(8,128)S(1)}) custom-call(bf16[64,576]{1,0:T(8,128)(2,1)S(1)} %copy-done, bf16[64,512]{1,0:T(8,128)(2,1)S(1)} %copy-done.1, bf16[2304,1024]{1,0:T(8,128)(2,1)} %tw_ref.1, bf16[2048,1024]{1,0:T(8,128)(2,1)} %sw_ref.1, s32[1,256]{1,0:T(1,128)S(1)} %bitcast.3), custom_call_target="tpu_custom_call" | custom-call | tf_op jit(solution)/shard_map/pallas_call | solution.py:373
  70.8 0.6 copy.11
  72.0 0.7 copy.13
Async XLA Ops:
  0.6 0.9 %copy-start = (bf16[64,576]{1,0:T(8,128)(2,1)S(1)}, bf16[64,576]{1,0:T(8,128)(2,1)}, u32[]{:S(2)}) copy-start(bf16[64,576]{1,0:T(8,128)(2,1)} %th_ref.1) | copy-start | bytes 221188
  1.5 0.8 %copy-start.1 = (bf16[64,512]{1,0:T(8,128)(2,1)S(1)}, bf16[64,512]{1,0:T(8,128)(2,1)}, u32[]{:S(2)}) copy-start(bf16[64,512]{1,0:T(8,128)(2,1)} %sh_ref.1) | copy-start | bytes 196612
  2.4 0.7 copy-start.2

commit v3 on v2

--- a/solution.py
+++ b/solution.py
@@ -147,22 +147,26 @@
     own_rows = pl.multiple_of(role * half, ROW_STEP)
     other_rows = pl.multiple_of((1 - role) * half, ROW_STEP)
 
+    early, late = ((1, 2), (3,)) if corner else ((), direct)
+    pass_on(teacher_part, 1)
+    relay(teacher_part, 0)
+    for j in range(2, dp_size):
+        pass_on(teacher_part, j)
+    relay(student_part, 0)
+    pass_on(student_part, 1)
     for j in range(1, dp_size):
-        pass_on(teacher_part, j)
+        relay(teacher_part, j)
+        if j + 1 < dp_size:
+            pass_on(student_part, j + 1)
     th_copy.wait()
     tw_copy.wait()
     add_product(th, tw, t_acc, 0)
-    relay(teacher_part, 0)
     for j in range(1, dp_size):
-        relay(teacher_part, j)
-        pass_on(student_part, j)
+        relay(student_part, j)
     sh_copy.wait()
     sw_copy.wait()
-    for j in range(dp_size):
-        relay(student_part, j)
+    add_arriving(teacher_part, tw, t_acc, early)
     add_product(sh, sw, s_acc, 0)
-    early, late = ((1, 2), (3,)) if corner else ((), direct)
-    add_arriving(teacher_part, tw, t_acc, early)
     add_arriving(student_part, sw, s_acc, early)
     add_arriving(teacher_part, tw, t_acc, late)
     send(t_acc.at[pl.ds(other_rows, half)], t_other, role_send.at[0], role_recv.at[0], partner)
@@ -289,18 +293,7 @@
                 h_send.at[0, 0, 0], h_recv.at[side, slot, dps[j]],
             )
 
-        for side in (0, 1):
-            out_hop[side, 1] = product(3, side, width).astype(HOP)
-            for j in far:
-                hop(side, 1, j)
-        for side in (0, 1):
-            out_hop[side, 0] = product(1 + side, side, width).astype(HOP)
-            hop(side, 0, far[0])
-        for side in (0, 1):
-            middle[side] = product(2 - side, side, width)
-        for side in (0, 1):
-            term[0, :, sides[side]] = product(0, side, width)
-        for at, j in enumerate(far):
+        def sum_middle(j):
             for side in (0, 1):
                 landed(in_hop, side, 1, j)
                 middle[side, block(j)] += in_hop[side, 1, block(j)].astype(jnp.float32)
@@ -309,10 +302,8 @@
                     h_send.at[side, 2, j], h_recv.at[side, 2, dps[j]],
                     (role, dp, vocabs[2 - side]),
                 )
-            if at + 1 < dp_size:
-                for side in (0, 1):
-                    hop(side, 0, far[at + 1])
-        for j in far:
+
+        def sum_last(j):
             totals = []
             for side in (0, 1):
                 landed(in_hop, side, 0, j)
@@ -320,6 +311,29 @@
                 landed(in_last, side, 2, j)
                 totals.append(near + in_last[side, block(j)])
             finish(j, jnp.concatenate(totals, axis=1))
+
+        for side in (0, 1):
+            out_hop[side, 1] = product(3, side, width).astype(HOP)
+            hop(side, 1, far[0])
+        for side in (0, 1):
+            out_hop[side, 0] = product(1 + side, side, width).astype(HOP)
+            hop(side, 0, far[0])
+            for j in far[1:2]:
+                hop(side, 1, j)
+        for side in (0, 1):
+            middle[side] = product(2 - side, side, width)
+        for side in (0, 1):
+            term[0, :, sides[side]] = product(0, side, width)
+        for at, j in enumerate(far):
+            sum_middle(j)
+            for side in (0, 1):
+                for later in far[at + 1:at + 2]:
+                    hop(side, 0, later)
+                for later in far[at + 2:at + 3]:
+                    hop(side, 1, later)
+            if at:
+                sum_last(far[at - 1])
+        sum_last(far[-1])
     else:
         width = min(TILE, features)
         order = list(range(vocab_size - 1, -1, -1))
@@ -346,7 +360,8 @@
 
     arrived(losses.at[1 - role], role_send.at[2], role_recv.at[2])
     both = losses[:, 0, :]
-    loss_ref[...] = both
+    loss_ref[:, 0:half] = both[0:1]
+    loss_ref[:, half:rows] = both[1:2]
     mean_ref[...] = jnp.sum(jnp.sum(both, axis=1, keepdims=True), axis=0, keepdims=True) * (1.0 / rows)
 
     for copy in sent:
@@ -373,7 +388,7 @@
     losses, mean, grad = pl.pallas_call(
         functools.partial(kernel, dp_size, vocab_size),
         out_shape=(
-            jax.ShapeDtypeStruct((2, half), f32),
+            jax.ShapeDtypeStruct((1, rows), f32),
             jax.ShapeDtypeStruct((1, 1), f32),
             jax.ShapeDtypeStruct((block_rows, s_depth), f32),
         ),

time: 74 us -> 72.6 us (0.981)
  Pallas kernels: 67.8 us -> 66.4 us
    pallas_call x1, Pallas kernels: 67.8 us -> 66.4 us  [per_device(): pl.pallas_call(functools.partial(kernel, dp_size, vocab_size), out_shape=...]
where the time goes in v3:
time: 72.6 us; the launch traced here: 72.4 us
  Pallas kernels  66.4 us (91%)
  local copies, waits for them, and re-layouts  3.62 us (5%)
  between operations  2.39 us (3%)
    pallas_call x1, Pallas kernels, per_device(): pl.pallas_call(functools.partial(kernel, dp_size, vocab_size), out_shape=...  66.4 us
    unnamed x8, local copies, waits for them, and re-layouts  3.62 us

profile of v3, /device:TPU:0, one launch (start us, length us, event | category | flops | bytes accessed | tf_op | source)
XLA Modules:
  0.0 72.4 jit_solution(13345754594413049277)
XLA Ops:
  0.6 0.0 copy-start
  0.6 0.9 %copy-done = bf16[64,576]{1,0:T(8,128)(2,1)S(1)} copy-done((bf16[64,576]{1,0:T(8,128)(2,1)S(1)}, bf16[64,576]{1,0:T(8,128)(2,1)}, u32[]{:S(2)}) %copy-start) | copy-done | bytes 73752
  1.5 0.0 copy-start.1
  1.5 0.8 %copy-done.1 = bf16[64,512]{1,0:T(8,128)(2,1)S(1)} copy-done((bf16[64,512]{1,0:T(8,128)(2,1)S(1)}, bf16[64,512]{1,0:T(8,128)(2,1)}, u32[]{:S(2)}) %copy-start.1) | copy-done | bytes 65560
  2.4 0.0 copy-start.2
  2.4 0.7 copy-done.2
  3.0 66.4 %shard_map.76 = (f32[1,256]{1,0:T(1,128)S(1)}, f32[1,1]{1,0:T(1,128)}, f32[64,512]{1,0:T(8,128)S(1)}) custom-call(bf16[64,576]{1,0:T(8,128)(2,1)S(1)} %copy-done, bf16[64,512]{1,0:T(8,128)(2,1)S(1)} %copy-done.1, bf16[2304,1024]{1,0:T(8,128)(2,1)} %tw_ref.1, bf16[2048,1024]{1,0:T(8,128)(2,1)} %sw_ref.1, s32[1,256]{1,0:T(1,128)S(1)} %bitcast.3), custom_call_target="tpu_custom_call" | custom-call | tf_op jit(solution)/shard_map/pallas_call | solution.py:388
  69.4 0.6 copy.11
  70.6 0.7 copy.13
Async XLA Ops:
  0.6 0.9 %copy-start = (bf16[64,576]{1,0:T(8,128)(2,1)S(1)}, bf16[64,576]{1,0:T(8,128)(2,1)}, u32[]{:S(2)}) copy-start(bf16[64,576]{1,0:T(8,128)(2,1)} %th_ref.1) | copy-start | bytes 221188
  1.5 0.8 %copy-start.1 = (bf16[64,512]{1,0:T(8,128)(2,1)S(1)}, bf16[64,512]{1,0:T(8,128)(2,1)}, u32[]{:S(2)}) copy-start(bf16[64,512]{1,0:T(8,128)(2,1)} %sh_ref.1) | copy-start | bytes 196612
  2.4 0.7 copy-start.2

commit v4 on v3

--- a/solution.py
+++ b/solution.py
@@ -239,19 +239,27 @@
     first = lax.broadcasted_iota(jnp.int32, (LANES, half), 0) == 0
     lse_col[...] = jnp.transpose(jnp.where(first, t_lse, s_lse))
 
-    @pl.loop(0, half // ROW_STEP)
-    def _(step):
-        local, whole = at_rows(step)
-        teacher = t_acc[whole, :] + t_other[local, :]
-        student = s_acc[whole, :] + s_other[local, :]
-        onehot = jnp.where(column == target_col[whole, 0:1], 1.0, 0.0)
-        t_prob = jnp.exp(teacher - lse_col[local, 0:1])
-        s_prob = jnp.exp(student - lse_col[local, 1:2])
-        logit_grad[whole, :] = (2.0 * s_prob - t_prob - onehot).astype(jnp.bfloat16)
-
-    mine = logit_grad.at[pl.ds(own_rows, half)]
-    send(mine, mine, role_send.at[3], role_recv.at[3], partner)
-    arrived(logit_grad.at[pl.ds(other_rows, half)], role_send.at[3], role_recv.at[3])
+    steps = half // ROW_STEP // 2
+    part_rows = steps * ROW_STEP
+
+    def grad_part(start, part):
+        return logit_grad.at[pl.ds(pl.multiple_of(start + part * part_rows, ROW_STEP), part_rows)]
+
+    for part in (0, 1):
+        @pl.loop(part * steps, (part + 1) * steps)
+        def _(step):
+            local, whole = at_rows(step)
+            teacher = t_acc[whole, :] + t_other[local, :]
+            student = s_acc[whole, :] + s_other[local, :]
+            onehot = jnp.where(column == target_col[whole, 0:1], 1.0, 0.0)
+            t_prob = jnp.exp(teacher - lse_col[local, 0:1])
+            s_prob = jnp.exp(student - lse_col[local, 1:2])
+            logit_grad[whole, :] = (2.0 * s_prob - t_prob - onehot).astype(jnp.bfloat16)
+
+        mine = grad_part(own_rows, part)
+        send(mine, mine, role_send.at[3 + part], role_recv.at[3 + part], partner)
+    for part in (0, 1):
+        arrived(grad_part(other_rows, part), role_send.at[0], role_recv.at[3 + part])
 
     def block(j):
         return pl.ds(pl.multiple_of(dps[j] * block_rows, block_rows), block_rows)
@@ -423,8 +431,8 @@
             dma((vocab_size, dp_size)),
             dma((vocab_size + 2, dp_size)),
             dma((vocab_size, dp_size)),
-            dma((4,)),
-            dma((4,)),
+            dma((5,)),
+            dma((5,)),
             dma((group,)),
             dma((group,)),
             dma((vocab_size, dp_size)),

time: 72.6 us -> 72.4 us (level)
  no operation moved by 1% of the time
where the time goes in v4:
time: 72.4 us; the launch traced here: 72.2 us
  Pallas kernels  66.2 us (91%)
  local copies, waits for them, and re-layouts  3.62 us (5%)
  between operations  2.39 us (3%)
    pallas_call x1, Pallas kernels, per_device(): pl.pallas_call(functools.partial(kernel, dp_size, vocab_size), out_shape=...  66.2 us
    unnamed x8, local copies, waits for them, and re-layouts  3.62 us

profile of v4, /device:TPU:0, one launch (start us, length us, event | category | flops | bytes accessed | tf_op | source)
XLA Modules:
  0.0 72.2 jit_solution(7530200809020256842)
XLA Ops:
  0.6 0.0 copy-start
  0.6 0.9 %copy-done = bf16[64,576]{1,0:T(8,128)(2,1)S(1)} copy-done((bf16[64,576]{1,0:T(8,128)(2,1)S(1)}, bf16[64,576]{1,0:T(8,128)(2,1)}, u32[]{:S(2)}) %copy-start) | copy-done | bytes 73752
  1.5 0.0 copy-start.1
  1.5 0.8 %copy-done.1 = bf16[64,512]{1,0:T(8,128)(2,1)S(1)} copy-done((bf16[64,512]{1,0:T(8,128)(2,1)S(1)}, bf16[64,512]{1,0:T(8,128)(2,1)}, u32[]{:S(2)}) %copy-start.1) | copy-done | bytes 65560
  2.4 0.0 copy-start.2
  2.4 0.7 copy-done.2
  3.0 66.2 %shard_map.76 = (f32[1,256]{1,0:T(1,128)S(1)}, f32[1,1]{1,0:T(1,128)}, f32[64,512]{1,0:T(8,128)S(1)}) custom-call(bf16[64,576]{1,0:T(8,128)(2,1)S(1)} %copy-done, bf16[64,512]{1,0:T(8,128)(2,1)S(1)} %copy-done.1, bf16[2304,1024]{1,0:T(8,128)(2,1)} %tw_ref.1, bf16[2048,1024]{1,0:T(8,128)(2,1)} %sw_ref.1, s32[1,256]{1,0:T(1,128)S(1)} %bitcast.3), custom_call_target="tpu_custom_call" | custom-call | tf_op jit(solution)/shard_map/pallas_call | solution.py:396
  69.2 0.6 copy.11
  70.4 0.7 copy.13
Async XLA Ops:
  0.6 0.9 %copy-start = (bf16[64,576]{1,0:T(8,128)(2,1)S(1)}, bf16[64,576]{1,0:T(8,128)(2,1)}, u32[]{:S(2)}) copy-start(bf16[64,576]{1,0:T(8,128)(2,1)} %th_ref.1) | copy-start | bytes 221188
  1.5 0.8 %copy-start.1 = (bf16[64,512]{1,0:T(8,128)(2,1)S(1)}, bf16[64,512]{1,0:T(8,128)(2,1)}, u32[]{:S(2)}) copy-start(bf16[64,512]{1,0:T(8,128)(2,1)} %sh_ref.1) | copy-start | bytes 196612
  2.4 0.7 copy-start.2
